TPU v7x, 32 devices: a whole 2x2x4 slice. The times are simulated.
32 devices in a mesh: dp: 8 (over z, x), own: 4 (over y, core).
Axes of the slice: x: 2, y: 2, z: 4, core: 2. Of those that a mesh axis runs over, the one named last changes fastest.
Arguments:
- grads: float32 [8, 4, 1024, 1024], P('dp', None, 'own'), may hold values from -0.27 to 0.27
- owner_map: int32 [4], replicated, may hold values from 0 to 7, as said below
- stat_left: float32 [8, 1024, 1024], P('own', 'dp'), as said below
- stat_right: float32 [8, 1024, 1024], P('own', 'dp'), as said below
- root_left: bfloat16 [8, 1024, 1024], P('own', 'dp'), as said below
- root_right: bfloat16 [8, 1024, 1024], P('own', 'dp'), as said below
- master: float32 [8, 1024, 1024], P('own', 'dp'), may hold values from -4 to 4
- moment_first: float32 [8, 1024, 1024], P('own', 'dp'), may hold values from -0.6 to 0.6
- moment_second: float32 [8, 1024, 1024], P('own', 'dp'), may hold values from 0.001 to 1, as said below
Outputs:
- left_next: float32 [8, 1024, 1024], P('own', 'dp')
- right_next: float32 [8, 1024, 1024], P('own', 'dp')
- master_next: float32 [8, 1024, 1024], P('own', 'dp')
- first_next: float32 [8, 1024, 1024], P('own', 'dp')
- second_next: float32 [8, 1024, 1024], P('own', 'dp')
- weights_out: bfloat16 [4, 1024, 1024], P(None, ('dp', 'own'))
Inputs may be any that keep to these rules, and one draw needn't show every extreme that they name: `owner_map`: no two blocks share a slot. In every draw all 2 slots of some owner are taken, and so are slots 0 and 7. `root_left`: symmetric in its last two dimensions. `root_right`: symmetric in its last two dimensions. `stat_left`: symmetric in its last two dimensions. `stat_right`: symmetric in its last two dimensions. `moment_second`: Positive.
All inputs are finite; a program needn't handle non-finite values.
Results may differ from a plain program's by a relative error of at most 0.0045.
Values may be sent and summed in bfloat16 or wider, within the bound.
A program may use at most 128 MiB of HBM per device.

v0:
```python
import jax
import jax.numpy as jnp
from jax import lax
from jax.sharding import PartitionSpec as P

stat_decay = 0.9
first_decay = 0.9
second_decay = 0.99
learn_rate = 0.25


def per_device(
    grads,
    owner_map,
    stat_left,
    stat_right,
    root_left,
    root_right,
    master,
    moment_first,
    moment_second,
):
    owners = lax.axis_size("own")
    slot_count = stat_left.shape[0]
    rows_dev = stat_left.shape[1]
    order_size = stat_left.shape[2]
    blocks = owner_map.shape[0]
    owned_slots = owners * slot_count
    highest = lax.Precision.HIGHEST
    matches = owner_map[:, None] == jnp.arange(owned_slots, dtype=jnp.int32)[None, :]
    occupied = jnp.any(matches, axis=0)
    block_of = jnp.sum(jnp.where(matches, jnp.arange(blocks, dtype=jnp.int32)[:, None], 0), axis=0)
    partials = grads[0]
    summed = lax.psum(partials, "dp")
    packed = jnp.where(occupied[:, None, None], jnp.take(summed, block_of, axis=0), 0.0)
    packed = packed.reshape(owners, slot_count, summed.shape[1], order_size)
    arrived = lax.all_to_all(
        packed.astype(jnp.bfloat16), "own", split_axis=0, concat_axis=2, tiled=True
    ).astype(packed.dtype)
    whole_grad = arrived.reshape(slot_count, order_size, order_size)
    first_row = lax.axis_index("dp") * rows_dev
    own_rows = lax.dynamic_slice_in_dim(whole_grad, first_row, rows_dev, 1)
    own_cols = lax.dynamic_slice_in_dim(whole_grad, first_row, rows_dev, 2)
    left_new = stat_decay * stat_left + (1.0 - stat_decay) * jnp.einsum(
        "srk,snk->srn", own_rows, whole_grad, precision=highest, preferred_element_type=jnp.float32
    )
    right_new = stat_decay * stat_right + (1.0 - stat_decay) * jnp.einsum(
        "skr,skn->srn", own_cols, whole_grad, precision=highest, preferred_element_type=jnp.float32
    )
    first_new = first_decay * moment_first + (1.0 - first_decay) * own_rows
    second_new = second_decay * moment_second + (1.0 - second_decay) * own_rows * own_rows
    adam_step = first_new / (jnp.sqrt(second_new) + 1e-08)
    rounded = whole_grad.astype(jnp.bfloat16)
    partial_product = jnp.einsum(
        "skn,srn->skr", rounded, root_right, preferred_element_type=jnp.float32
    ).astype(jnp.bfloat16)
    direction = jnp.einsum(
        "srk,skn->srn",
        root_left,
        lax.all_gather(partial_product, "dp", axis=2, tiled=True),
        preferred_element_type=jnp.float32,
    )
    square_sums = lax.psum(
        (jnp.sum(adam_step * adam_step, axis=(1, 2)), jnp.sum(direction * direction, axis=(1, 2))),
        "dp",
    )
    graft = jnp.sqrt(square_sums[0]) / (jnp.sqrt(square_sums[1]) + 1e-06)
    master_new = master - learn_rate * graft[:, None, None] * direction
    occupied_mine = lax.dynamic_slice_in_dim(
        occupied, lax.axis_index("own") * slot_count, slot_count
    )[:, None, None]
    left_next = jnp.where(occupied_mine, left_new, stat_left)
    right_next = jnp.where(occupied_mine, right_new, stat_right)
    master_next = jnp.where(occupied_mine, master_new, master)
    first_next = jnp.where(occupied_mine, first_new, moment_first)
    second_next = jnp.where(occupied_mine, second_new, moment_second)
    shares = master_new.astype(jnp.bfloat16).reshape(
        slot_count, owners, rows_dev // owners, order_size
    )
    delivered = lax.all_to_all(shares, "own", split_axis=1, concat_axis=0, tiled=True)
    delivered = delivered.reshape(owned_slots, rows_dev // owners, order_size)
    weights_out = jnp.take(delivered, owner_map, axis=0)
    return (left_next, right_next, master_next, first_next, second_next, weights_out)


def solution(mesh):
    return jax.shard_map(
        per_device,
        mesh=mesh,
        in_specs=(
            P("dp", None, "own", None),
            P(),
            P("own", "dp", None),
            P("own", "dp", None),
            P("own", "dp", None),
            P("own", "dp", None),
            P("own", "dp", None),
            P("own", "dp", None),
            P("own", "dp", None),
        ),
        out_specs=(
            P("own", "dp", None),
            P("own", "dp", None),
            P("own", "dp", None),
            P("own", "dp", None),
            P("own", "dp", None),
            P(None, ("dp", "own"), None),
        ),
        check_vma=False,
    )
```

profile of v0, /device:TPU:1, one launch (start us, length us, event | category | flops | bytes accessed | tf_op | source)
XLA Modules:
  0.0 355.7 jit_solution(14918357221565450593)
XLA Ops:
  7.2 0.0 copy-start
  7.2 0.0 all-gather.2.cloned.1.call-start
  7.2 0.8 fusion.13
  8.0 0.7 select_reduce_fusion
  8.8 0.1 reduce_sum.32
  8.8 0.1 broadcast_in_dim.75
  9.0 167.6 %all-reduce.2 = bf16[4,256,1024]{2,1,0:T(8,128)(2,1)S(1)} all-reduce(f32[4,256,1024]{2,1,0:T(8,128)} %bitcast.53), channel_id=1, replica_groups=mesh['dp'=8,'own'=4] {'dp'}, use_global_device_ids=true, to_apply=%region_2.3 | all-reduce | flops 1048576 | bytes 6291456 | tf_op jit(solution)/shard_map/psum | solution.py:34
  176.6 2.8 gather_fusion
  179.3 3.6 %select_convert_fusion = bf16[4,2,256,1024]{3,2,1,0:T(8,128)(2,1)S(1)} fusion(bf16[4,2,256,1024]{3,2,1,0:T(8,128)(2,1)} %bitcast.52, pred[4,2]{1,0:T(4,128)(4,1)S(1)} %compare_and_fusion.1, pred[4,2]{1,0:T(4,128)(4,1)S(1)} %broadcast_in_dim.75), kind=kLoop, calls=%fused_computation.2 | loop fusion | flops 4194304 | bytes 8388624 | tf_op jit(solution)/shard_map/convert_element_type | solution.py:38
  183.0 50.7 %all_to_all.30 = bf16[4,2,256,1024]{3,2,1,0:T(8,128)(2,1)S(1)} all-to-all(bf16[4,2,256,1024]{3,2,1,0:T(8,128)(2,1)S(1)} %select_convert_fusion), channel_id=1, replica_groups=mesh['dp'=8,'own'=4] {'own'}, dimensions={0} | all-to-all | bytes 8388608 | tf_op jit(solution)/shard_map/all_to_all | solution.py:37
  233.7 0.0 copy-start.7
  233.7 0.4 copy.30
  234.2 0.0 copy-start.1
  234.2 0.0 copy-start.8
  234.2 0.0 copy-start.4
  234.2 0.0 copy-start.5
  234.2 2.1 copy-done.1
  236.3 0.0 copy-done.7
  236.3 2.0 convolution_convert_fusion
  238.4 0.0 all-gather.2.cloned.1.call-update
  238.4 0.1 dynamic_slice.13
  238.5 0.0 copy-done.8
  238.5 0.0 copy-done.4
  238.5 0.0 copy-done.5
  238.5 3.4 fusion.7
  241.9 0.0 copy-start.6
  241.9 69.3 %all-gather.2.cloned.1.call-done = bf16[2,1024,1024]{2,1,0:T(8,128)(2,1)} async-done(((bf16[2,1024,128]{2,1,0:T(8,128)(2,1)}), bf16[2,1024,1024]{2,1,0:T(8,128)(2,1)}) %all-gather.2.cloned.1.call-update) | async-done | bytes 4194320 | tf_op jit(solution)/shard_map/all_gather | solution.py:60
  311.2 0.0 copy-done
  311.2 3.0 multiply_reduce_fusion
  314.3 15.5 %all-reduce = (f32[2]{0:T(128)S(1)}, f32[2]{0:T(128)S(1)}) all-reduce(f32[2]{0:T(128)S(1)} %get-tuple-element.13, f32[2]{0:T(128)S(1)} %get-tuple-element.9), channel_id=1, replica_groups=mesh['dp'=8,'own'=4] {'dp'}, use_global_device_ids=true, to_apply=%region_6.7 | all-reduce | flops 4 | bytes 32 | tf_op jit(solution)/shard_map/psum | solution.py:63
  329.8 0.0 copy-done.6
  329.8 1.3 fusion.9
  331.0 0.0 copy-start.3
  331.0 0.8 copy.32
  331.9 7.6 %all-to-all-start.1 = ((bf16[2,4,32,1024]{3,2,0,1:T(8,128)(2,1)}), bf16[2,4,32,1024]{3,2,0,1:T(8,128)(2,1)S(1)}, u32[]{:S(2)}, u32[]{:S(2)}) async-start(bf16[2,4,32,1024]{3,2,0,1:T(8,128)(2,1)} %copy.32), calls=%async_computation.1 | async-start | bytes 1048576 | tf_op jit(solution)/shard_map/all_to_all | solution.py:80
  339.5 0.0 copy-start.2
  339.5 5.3 %fusion.3 = f32[2,128,1024]{2,1,0:T(8,128)} fusion(f32[2,128,1024]{2,1,0:T(8,128)} %param.11, bf16[2,1024,1024]{2,1,0:T(8,128)(2,1)} %bitcast.50, s32[]{:T(128)S(6)} %select_n.69, pred[2]{0:T(512)(128)(4,1)S(1)} %dynamic_slice.13), kind=kOutput, calls=%fused_computation.9 | convolution fusion | flops 537919488 | bytes 6815750 | tf_op jit(solution)/shard_map/srk,snk->srn/dot_general | solution.py:44
  344.8 0.0 copy-done.3
  344.8 0.0 copy-done.2
  344.8 1.9 fusion.1
  346.7 0.7 all-to-all-done.1
  347.5 0.6 gather_fusion.1
  348.0 0.8 broadcast_select_fusion
  (7 shorter events, 0.1 us)
Async XLA Ops:
  7.2 304.1 %copy-start = (bf16[2,128,1024]{2,1,0:T(8,128)(2,1)S(1)}, bf16[2,128,1024]{2,1,0:T(8,128)(2,1)}, u32[]{:S(2)}) copy-start(bf16[2,128,1024]{2,1,0:T(8,128)(2,1)} %param.13) | copy-start | bytes 1572868
  7.2 304.1 %all-gather.2.cloned.1.call-start = ((), (), s32[]{:S(2)}) async-start(), calls=%async_computation.2 | async-start | bytes 4718592 | tf_op jit(solution)/shard_map/all_gather | solution.py:60
  233.7 2.6 copy-start.7
  234.2 2.1 copy-start.1
  234.2 4.3 %copy-start.8 = (s32[4]{0:T(128)S(1)}, s32[4]{0:T(128)}, u32[]{:S(2)}) copy-start(s32[4]{0:T(128)} %param.10) | copy-start | bytes 52
  234.2 4.3 %copy-start.4 = (f32[2,128,1024]{2,1,0:T(8,128)S(1)}, f32[2,128,1024]{2,1,0:T(8,128)}, u32[]{:S(2)}) copy-start(f32[2,128,1024]{2,1,0:T(8,128)} %param.17) | copy-start | bytes 3145732
  234.2 4.3 %copy-start.5 = (f32[2,128,1024]{2,1,0:T(8,128)S(1)}, f32[2,128,1024]{2,1,0:T(8,128)}, u32[]{:S(2)}) copy-start(f32[2,128,1024]{2,1,0:T(8,128)} %param.16) | copy-start | bytes 3145732
  241.9 87.9 %copy-start.6 = (f32[2,128,1024]{2,1,0:T(8,128)S(1)}, f32[2,128,1024]{2,1,0:T(8,128)}, u32[]{:S(2)}) copy-start(f32[2,128,1024]{2,1,0:T(8,128)} %param.15) | copy-start | bytes 3145732
  331.0 13.8 %copy-start.3 = (f32[2,128,1024]{2,1,0:T(8,128)S(1)}, f32[2,128,1024]{2,1,0:T(8,128)}, u32[]{:S(2)}) copy-start(f32[2,128,1024]{2,1,0:T(8,128)} %param.12) | copy-start | bytes 3145732
  331.9 15.6 %all-to-all-start.1 = ((bf16[2,4,32,1024]{3,2,0,1:T(8,128)(2,1)}), bf16[2,4,32,1024]{3,2,0,1:T(8,128)(2,1)S(1)}, u32[]{:S(2)}, u32[]{:S(2)}) async-start(bf16[2,4,32,1024]{3,2,0,1:T(8,128)(2,1)} %copy.32), calls=%async_computation.1 | async-start | bytes 1048576 | tf_op jit(solution)/shard_map/all_to_all | solution.py:80
  339.5 5.3 %copy-start.2 = (bf16[4,2,256,1024]{3,2,0,1:T(8,128)(2,1)S(1)}, bf16[4,2,256,1024]{3,2,0,1:T(8,128)(2,1)}, u32[]{:S(2)}) copy-start(bf16[4,2,256,1024]{3,2,0,1:T(8,128)(2,1)} %copy-done.1) | copy-start | bytes 12582916
Sparse Core Ops, SparseCore 0:
  238.5 72.6 all-gather.1
where the time goes:
time: 357 us; the launch traced here: 356 us
  blocking collectives  234 us (66%)
  waiting for transfers between devices  70.1 us (20%)
  between operations  14.2 us (4%)
  matrix products  12.3 us (3%)
  other arithmetic  10.7 us (3%)
  starting transfers between devices  7.66 us (2%)
  local copies, waits for them, and re-layouts  6.96 us (2%)
    psum x1, blocking collectives, per_device(): summed = lax.psum(partials, 'dp')  168 us
    all_gather x1, waiting for transfers between devices, per_device(): lax.all_gather(partial_product, 'dp', axis=2, tiled=True)  69.3 us
    all_to_all x1, blocking collectives, per_device(): lax.all_to_all(packed.astype(jnp.bfloat16), 'own', split_axis=0, concat_a...  50.7 us
    psum x1, blocking collectives, per_device(): lax.psum((jnp.sum(adam_step * adam_step, axis=(1, 2)), jnp.sum(direction...  15.5 us
    all_to_all x1, starting transfers between devices, per_device(): lax.all_to_all(shares, 'own', split_axis=1, concat_axis=0, tiled=True)  7.62 us
  transfers between devices with their start and end apart: 2, of which 2 were waited for; matrix products, arithmetic and copies ran while one was open for 3% of the time, Pallas kernels for 0%

commit v1 on v0

v1 whole, which is shorter than its diff:
```python
import functools

import jax
import jax.numpy as jnp
from jax import lax
from jax.experimental import pallas as pl
from jax.experimental.pallas import tpu as pltpu
from jax.sharding import PartitionSpec as P

stat_decay = 0.9
first_decay = 0.9
second_decay = 0.99
learn_rate = 0.25

VM = pltpu.VMEM
MIB = 1 << 20


def remote(src, dst, send, recv, dp, own):
    return pltpu.make_async_remote_copy(
        src_ref=src,
        dst_ref=dst,
        send_sem=send,
        recv_sem=recv,
        device_id=(dp, own),
        device_id_type=pl.DeviceIdType.MESH,
    )


def greet(dps, owns):
    dp, own = lax.axis_index("dp"), lax.axis_index("own")
    barrier = pltpu.get_barrier_semaphore()
    for k in range(1, dps):
        pl.semaphore_signal(barrier, inc=1, device_id=(lax.rem(dp + k, dps), own), device_id_type=pl.DeviceIdType.MESH)
    for k in range(1, owns):
        pl.semaphore_signal(barrier, inc=1, device_id=(dp, lax.rem(own + k, owns)), device_id_type=pl.DeviceIdType.MESH)
    pl.semaphore_wait(barrier, dps + owns - 2)


class Gather:
    def __init__(self, piece, nz, sems):
        self.piece, self.nz = piece, nz
        self.zs, self.zr, self.xs, self.xr = sems
        dp = lax.axis_index("dp")
        self.own = lax.axis_index("own")
        self.z, self.x = dp // 2, lax.rem(dp, 2)

    def along(self, way, t):
        sign = 1 - 2 * way
        at = self.z - sign * t
        there = self.z + sign
        ok = (at >= 0) & (at < self.nz) & (there >= 0) & (there < self.nz)
        ref = self.piece(at * 2 + self.x)
        return ok, remote(ref, ref, self.zs.at[way, t], self.zr.at[way, t], there * 2 + self.x, self.own)

    def across(self, way, t):
        sign = 1 - 2 * way
        at = self.z - sign * t
        ok = (at >= 0) & (at < self.nz)
        ref = self.piece(at * 2 + self.x)
        return ok, remote(ref, ref, self.xs.at[way, t], self.xr.at[way, t], self.z * 2 + 1 - self.x, self.own)

    def came(self, way, t):
        sign = 1 - 2 * way
        at = self.z - sign * (t + 1)
        ok = (at >= 0) & (at < self.nz)
        ref = self.piece(at * 2 + self.x)
        return ok, remote(ref, ref, self.zs.at[way, t], self.zr.at[way, t], self.z * 2 + 1 - self.x, self.own)

    def crossed(self, way, t):
        sign = 1 - 2 * way
        at = self.z - sign * t
        ok = (at >= 0) & (at < self.nz)
        ref = self.piece(at * 2 + 1 - self.x)
        return ok, remote(ref, ref, self.xs.at[way, t], self.xr.at[way, t], self.z * 2 + 1 - self.x, self.own)

    def start(self):
        for way in range(2):
            ok, copy = self.along(way, 0)
            pl.when(ok)(copy.start)
        self.across(0, 0)[1].start()

    def step(self, t):
        for way in range(2):
            ok, copy = self.came(way, t)
            pl.when(ok)(copy.wait_recv)
            if t + 1 < self.nz - 1:
                ok, copy = self.along(way, t + 1)
                pl.when(ok)(copy.start)
            ok, copy = self.across(way, t + 1)
            pl.when(ok)(copy.start)

    def finish(self):
        for t in range(self.nz):
            for way in range(1 if t == 0 else 2):
                ok, copy = self.crossed(way, t)
                pl.when(ok)(copy.wait_recv)
                ok, copy = self.across(way, t)
                pl.when(ok)(copy.wait_send)
        for t in range(self.nz - 1):
            for way in range(2):
                ok, copy = self.along(way, t)
                pl.when(ok)(copy.wait_send)


def exchange_kernel(
    dps, owns, blocks, slots, part,
    pick, grad, root, whole, roots,
    landed, packed, p_send, p_recv, o_send, o_recv,
    gzs, gzr, gxs, gxr, rzs, rzr, rxs, rxr, own_sem,
):
    dp, own = lax.axis_index("dp"), lax.axis_index("own")
    nz = dps // 2
    mine = pltpu.make_async_copy(root, roots.at[:, dp], own_sem)
    mine.start()
    greet(dps, owns)

    def scatter(k):
        there = lax.rem(dp + k, dps)
        rows = pl.ds(pl.multiple_of(there * part, part), part)
        return remote(grad.at[:, rows, :], landed.at[k - 1], p_send.at[k - 1], p_recv.at[k - 1], there, own)

    for k in range(1, dps):
        scatter(k).start()
    mine.wait()
    fetch = Gather(lambda at: roots.at[:, at], nz, (rzs, rzr, rxs, rxr))
    fetch.start()
    for t in range(nz - 2):
        fetch.step(t)
    for k in range(1, dps):
        scatter(k).wait_recv()
    rows = pl.ds(pl.multiple_of(dp * part, part), part)
    for b in range(blocks):
        total = grad[b, rows, :].astype(jnp.float32)
        for k in range(1, dps):
            total = total + landed[k - 1, b].astype(jnp.float32)
        packed[owns * slots + b] = total.astype(jnp.bfloat16)
    for s in range(owns * slots):
        total = pick[s] * packed[owns * slots].astype(jnp.float32)
        for b in range(1, blocks):
            total = total + pick[b * owns * slots + s] * packed[owns * slots + b].astype(jnp.float32)
        packed[s] = total.astype(jnp.bfloat16)

    def deliver(k):
        there = lax.rem(own + k, owns)
        return remote(
            packed.at[pl.ds(there * slots, slots)], whole.at[:, own, dp], o_send.at[k - 1], o_recv.at[k - 1], dp, there
        )

    def delivered(k):
        source = lax.rem(own + owns - k, owns)
        return remote(
            packed.at[pl.ds(own * slots, slots)], whole.at[:, source, dp], o_send.at[k - 1], o_recv.at[k - 1], dp, lax.rem(own + k, owns)
        )

    for k in range(1, owns):
        deliver(k).start()
    for s in range(slots):
        whole[s, own, dp] = packed[own * slots + s]
    fetch.step(nz - 2)
    for k in range(1, owns):
        delivered(k).wait_recv()
    spread = Gather(lambda at: whole.at[:, :, at], nz, (gzs, gzr, gxs, gxr))
    spread.start()
    for t in range(nz - 1):
        spread.step(t)
    fetch.finish()
    spread.finish()
    for k in range(1, owns):
        deliver(k).wait_send()
    for k in range(1, dps):
        scatter(k).wait_send()


def exchange(pick, grad, root, dps, owns):
    blocks, rows, cols = grad.shape
    slots, rows_dev = root.shape[:2]
    part = rows // dps
    nz = dps // 2
    dma = pltpu.SemaphoreType.DMA
    return pl.pallas_call(
        functools.partial(exchange_kernel, dps, owns, blocks, slots, part),
        out_shape=(
            jax.ShapeDtypeStruct((slots, owns, dps, part, cols), jnp.bfloat16),
            jax.ShapeDtypeStruct((slots, dps, rows_dev, cols), jnp.bfloat16),
        ),
        in_specs=[pl.BlockSpec(memory_space=pltpu.SMEM)] + [pl.BlockSpec(memory_space=VM)] * 2,
        out_specs=(pl.BlockSpec(memory_space=VM),) * 2,
        scratch_shapes=[
            VM((dps - 1, blocks, part, cols), jnp.bfloat16),
            VM((owns * slots + blocks, part, cols), jnp.bfloat16),
            dma((dps - 1,)),
            dma((dps - 1,)),
            dma((owns - 1,)),
            dma((owns - 1,)),
        ]
        + [dma((2, nz))] * 8
        + [dma],
        compiler_params=pltpu.CompilerParams(collective_id=0, has_side_effects=True, vmem_limit_bytes=40 * MIB),
    )(pick, grad, root)


def finish_kernel(dps, owns, slots, part, squares, direction, master, sums, out, held, shares, s_send, s_recv, w_send, w_recv):
    dp, own = lax.axis_index("dp"), lax.axis_index("own")
    greet(dps, owns)

    def tell(k):
        return remote(squares, held.at[k - 1], s_send.at[k - 1], s_recv.at[k - 1], lax.rem(dp + k, dps), own)

    for k in range(1, dps):
        tell(k).start()
    for k in range(1, dps):
        tell(k).wait_recv()
    total = squares[...]
    for k in range(1, dps):
        total = total + held[k - 1]
    sums[...] = total
    for s in range(slots):
        graft = jnp.sqrt(total[s : s + 1, :1]) / (jnp.sqrt(total[slots + s : slots + s + 1, :1]) + 1e-06)
        for o in range(owns):
            rows = pl.ds(o * part, part)
            shares[o, s] = (master[s, rows, :] - learn_rate * graft * direction[s, rows, :]).astype(jnp.bfloat16)

    def deliver(k):
        there = lax.rem(own + k, owns)
        return remote(shares.at[there], out.at[own], w_send.at[k - 1], w_recv.at[k - 1], dp, there)

    def delivered(k):
        source = lax.rem(own + owns - k, owns)
        return remote(shares.at[own], out.at[source], w_send.at[k - 1], w_recv.at[k - 1], dp, lax.rem(own + k, owns))

    for k in range(1, owns):
        deliver(k).start()
    out[own] = shares[own]
    for k in range(1, owns):
        delivered(k).wait_recv()
    for k in range(1, owns):
        deliver(k).wait_send()
    for k in range(1, dps):
        tell(k).wait_send()


def finish(squares, direction, master, dps, owns):
    slots, rows_dev, cols = master.shape
    part = rows_dev // owns
    dma = pltpu.SemaphoreType.DMA
    return pl.pallas_call(
        functools.partial(finish_kernel, dps, owns, slots, part),
        out_shape=(
            jax.ShapeDtypeStruct(squares.shape, jnp.float32),
            jax.ShapeDtypeStruct((owns, slots, part, cols), jnp.bfloat16),
        ),
        in_specs=[pl.BlockSpec(memory_space=VM)] * 3,
        out_specs=(pl.BlockSpec(memory_space=VM),) * 2,
        scratch_shapes=[
            VM((dps - 1,) + squares.shape, jnp.float32),
            VM((owns, slots, part, cols), jnp.bfloat16),
            dma((dps - 1,)),
            dma((dps - 1,)),
            dma((owns - 1,)),
            dma((owns - 1,)),
        ],
        compiler_params=pltpu.CompilerParams(collective_id=1, has_side_effects=True, vmem_limit_bytes=24 * MIB),
    )(squares, direction, master)


def whole_by_collectives(grads, owner_map, root_right, occupied, block_of):
    owners = lax.axis_size("own")
    slot_count, _, order_size = root_right.shape
    summed = lax.psum(grads[0], "dp")
    packed = jnp.stack(
        [lax.dynamic_index_in_dim(summed, block_of[s], 0, keepdims=False) for s in range(owners * slot_count)]
    )
    packed = jnp.where(occupied[:, None, None], packed, 0.0)
    packed = packed.reshape(owners, slot_count, summed.shape[1], order_size).astype(jnp.bfloat16)
    arrived = lax.all_to_all(packed, "own", split_axis=0, concat_axis=2, tiled=True)
    return (
        arrived.reshape(slot_count, order_size, order_size),
        lax.all_gather(root_right, "dp", axis=1, tiled=True),
    )


def per_device(
    grads,
    owner_map,
    stat_left,
    stat_right,
    root_left,
    root_right,
    master,
    moment_first,
    moment_second,
):
    owners, groups = lax.axis_size("own"), lax.axis_size("dp")
    slot_count, rows_dev, order_size = stat_left.shape
    blocks = owner_map.shape[0]
    owned_slots = owners * slot_count
    matches = owner_map[:, None] == jnp.arange(owned_slots, dtype=jnp.int32)[None, :]
    occupied = jnp.any(matches, axis=0)
    kernels = groups % 2 == 0 and (grads.shape[2] // groups) % 16 == 0 and (rows_dev // owners) % 16 == 0
    if kernels:
        pick = matches.astype(jnp.float32).reshape(-1)
        whole, right = exchange(pick, grads[0].astype(jnp.bfloat16), root_right, groups, owners)
        whole = whole.reshape(slot_count, order_size, order_size)
        right = right.reshape(slot_count, order_size, order_size)
    else:
        block_of = jnp.sum(jnp.where(matches, jnp.arange(blocks, dtype=jnp.int32)[:, None], 0), axis=0)
        whole, right = whole_by_collectives(grads, owner_map, root_right, occupied, block_of)
    first_row = lax.axis_index("dp") * rows_dev
    own_rows = lax.dynamic_slice_in_dim(whole, first_row, rows_dev, 1)
    own_cols = lax.dynamic_slice_in_dim(whole, first_row, rows_dev, 2)
    mixed = jnp.einsum("srk,skn->srn", root_left, whole, preferred_element_type=jnp.float32)
    direction = jnp.einsum(
        "srk,skn->srn", mixed.astype(jnp.bfloat16), right, preferred_element_type=jnp.float32
    )
    rows32 = own_rows.astype(jnp.float32)
    first_new = first_decay * moment_first + (1.0 - first_decay) * rows32
    second_new = second_decay * moment_second + (1.0 - second_decay) * rows32 * rows32
    adam_step = first_new / (jnp.sqrt(second_new) + 1e-08)
    square_sums = jnp.concatenate(
        [jnp.sum(adam_step * adam_step, axis=(1, 2)), jnp.sum(direction * direction, axis=(1, 2))]
    )
    if kernels:
        padded = jnp.pad(square_sums, (0, -2 * slot_count % 8))
        totals, delivered = finish(
            jnp.broadcast_to(padded[:, None], (padded.shape[0], 128)), direction, master, groups, owners
        )
        square_sums = totals[: 2 * slot_count, 0]
    else:
        square_sums = lax.psum(square_sums, "dp")
    graft = jnp.sqrt(square_sums[:slot_count]) / (jnp.sqrt(square_sums[slot_count:]) + 1e-06)
    master_new = master - learn_rate * graft[:, None, None] * direction
    if not kernels:
        shares = master_new.astype(jnp.bfloat16).reshape(slot_count, owners, rows_dev // owners, order_size)
        delivered = lax.all_to_all(shares, "own", split_axis=1, concat_axis=0, tiled=True)
    delivered = delivered.reshape(owned_slots, rows_dev // owners, order_size)
    left_new = stat_decay * stat_left + (1.0 - stat_decay) * jnp.einsum(
        "srk,snk->srn", own_rows, whole, preferred_element_type=jnp.float32
    )
    right_new = stat_decay * stat_right + (1.0 - stat_decay) * jnp.einsum(
        "skr,skn->srn", own_cols, whole, preferred_element_type=jnp.float32
    )
    occupied_mine = lax.dynamic_slice_in_dim(
        occupied, lax.axis_index("own") * slot_count, slot_count
    )[:, None, None]
    left_next = jnp.where(occupied_mine, left_new, stat_left)
    right_next = jnp.where(occupied_mine, right_new, stat_right)
    master_next = jnp.where(occupied_mine, master_new, master)
    first_next = jnp.where(occupied_mine, first_new, moment_first)
    second_next = jnp.where(occupied_mine, second_new, moment_second)
    weights_out = jnp.stack(
        [lax.dynamic_index_in_dim(delivered, owner_map[b], 0, keepdims=False) for b in range(blocks)]
    )
    return (left_next, right_next, master_next, first_next, second_next, weights_out)


def solution(mesh):
    state = P("own", "dp", None)
    return jax.shard_map(
        per_device,
        mesh=mesh,
        in_specs=(P("dp", None, "own", None), P()) + (state,) * 7,
        out_specs=(state,) * 5 + (P(None, ("dp", "own"), None),),
        check_vma=False,
    )
```

time: 357 us -> 192 us (0.54)
  blocking collectives: 234 us -> 0 us
  Pallas kernels: 0 us -> 158 us
  waiting for transfers between devices: 70.1 us -> 0 us
  starting transfers between devices: 7.66 us -> 0 us
  between operations: 14.2 us -> 8.5 us
    psum x2 -> x0, blocking collectives: 183 us -> none  [the longest x1 168 us: per_device(): summed = lax.psum(partials, 'dp')]
    pallas_call x0 -> x2, Pallas kernels: none -> 158 us  [the longest x1 142 us: exchange(): pl.pallas_call(functools.partial(exchange_kernel, dps, owns, blocks, slot...]
    all_gather x1 -> x0, waiting for transfers between devices: 69.3 us -> none  [per_device(): lax.all_gather(partial_product, 'dp', axis=2, tiled=True)]
    all_to_all x1 -> x0, blocking collectives: 50.7 us -> none  [per_device(): lax.all_to_all(packed.astype(jnp.bfloat16), 'own', split_axis=0, concat_a...]
    all_to_all x1 -> x0, starting transfers between devices: 7.62 us -> none  [per_device(): lax.all_to_all(shares, 'own', split_axis=1, concat_axis=0, tiled=True)]
    dot_general x4 -> x3, matrix products: 12.3 us -> 11.9 us  [the longest x1 4.93 us: per_device(): jnp.einsum('srk,skn->srn', mixed.astype(jnp.bfloat16), right, preferred_e...]
  transfers between devices with their start and end apart: 2 -> 0, of which waited for: 2 -> 0; matrix products, arithmetic and copies ran while one was open for 3% -> 0% of each run, Pallas kernels for 0% -> 0%
where the time goes in v1:
time: 192 us; the launch traced here: 191 us
  Pallas kernels  158 us (82%)
  matrix products  11.9 us (6%)
  between operations  8.5 us (4%)
  other arithmetic  7.76 us (4%)
  local copies, waits for them, and re-layouts  5.59 us (3%)
    pallas_call x1, Pallas kernels, exchange(): pl.pallas_call(functools.partial(exchange_kernel, dps, owns, blocks, slot...  142 us
    pallas_call x1, Pallas kernels, finish(): pl.pallas_call(functools.partial(finish_kernel, dps, owns, slots, part),...  16 us
    dot_general x1, matrix products, per_device(): jnp.einsum('srk,skn->srn', mixed.astype(jnp.bfloat16), right, preferred_e...  4.93 us
    dot_general x1, matrix products, per_device(): jnp.einsum('skr,skn->srn', own_cols, whole, preferred_element_type=jnp.fl...  4.43 us
    unnamed x20, local copies, waits for them, and re-layouts  3.94 us

profile of v1, /device:TPU:1, one launch (start us, length us, event | category | flops | bytes accessed | tf_op | source)
XLA Modules:
  0.0 191.3 jit_solution(9289980313223130987)
XLA Ops:
  0.6 0.0 copy-start
  0.6 0.0 copy-start.5
  0.7 1.4 fusion.16
  9.8 0.7 fusion.12
  10.6 0.1 dynamic_slice.22
  10.6 0.1 reshape.57.pick
  10.7 2.5 %convert_bitcast_fusion.grad = bf16[4,256,1024]{2,1,0:T(8,128)(2,1)S(1)} fusion(f32[1,4,256,1024]{3,2,1,0:T(8,128)} %param.9), kind=kLoop, calls=%fused_computation | loop fusion | flops 1048576 | bytes 6291456 | tf_op jit(solution)/shard_map/convert_element_type | solution.py:303
  13.2 0.0 copy-done.5
  13.3 141.5 %shard_map.136 = (bf16[2,4,8,32,1024]{4,3,2,1,0:T(8,128)(2,1)S(1)}, bf16[2,8,128,1024]{3,2,1,0:T(8,128)(2,1)S(1)}) custom-call(f32[32]{0:T(128)S(1)} %reshape.57.pick, bf16[4,256,1024]{2,1,0:T(8,128)(2,1)S(1)} %convert_bitcast_fusion.grad, bf16[2,128,1024]{2,1,0:T(8,128)(2,1)S(1)} %copy-done.5), custom_call_target="tpu_custom_call" | custom-call | tf_op jit(solution)/shard_map/pallas_call | solution.py:181
  154.8 0.0 copy-start.1
  154.8 1.9 %copy-done.1 = bf16[2,4,8,32,1024]{4,3,2,1,0:T(8,128)(2,1)} copy-done((bf16[2,4,8,32,1024]{4,3,2,1,0:T(8,128)(2,1)}, bf16[2,4,8,32,1024]{4,3,2,1,0:T(8,128)(2,1)S(1)}, u32[]{:S(2)}) %copy-start.1) | copy-done | bytes 4194328
  156.7 0.0 copy-start.3
  156.7 2.0 %copy-done.3 = bf16[2,8,128,1024]{3,2,1,0:T(8,128)(2,1)} copy-done((bf16[2,8,128,1024]{3,2,1,0:T(8,128)(2,1)}, bf16[2,8,128,1024]{3,2,1,0:T(8,128)(2,1)S(1)}, u32[]{:S(2)}) %copy-start.3) | copy-done | bytes 4194328
  158.7 0.0 copy-done
  158.7 0.0 copy-start.6
  158.7 4.9 %multiply_reduce_fusion = (f32[2]{0:T(128)S(1)}, f32[2,128,1024]{2,1,0:T(8,128)S(1)}) fusion(bf16[2,1024,1024]{2,1,0:T(8,128)(2,1)} %bitcast.18, bf16[2,128,1024]{2,1,0:T(8,128)(2,1)S(1)} %copy-done, bf16[2,1024,1024]{2,1,0:T(8,128)(2,1)} %bitcast.14), kind=kOutput, calls=%fused_computation.14 | convolution fusion | flops 1074528256 | bytes 9961480 | tf_op jit(solution)/shard_map/srk,skn->srn/dot_general | solution.py:313
  163.6 0.0 copy-done.6
  163.6 0.0 copy-start.2
  163.6 0.0 copy-start.7
  163.6 4.4 %fusion.1 = f32[2,128,1024]{2,1,0:T(8,128)} fusion(f32[2,128,1024]{2,1,0:T(8,128)S(1)} %copy-done.6, bf16[2,1024,1024]{2,1,0:T(8,128)(2,1)} %bitcast.15, s32[]{:T(128)S(6)} %select_n.37, pred[2]{0:T(512)(128)(4,1)S(1)} %dynamic_slice.22), kind=kOutput, calls=%fused_computation.5 | convolution fusion | flops 537919488 | bytes 6815750 | tf_op jit(solution)/shard_map/skr,skn->srn/dot_general | solution.py:340
  168.1 0.0 copy-done.2
  168.1 0.0 copy-done.7
  168.1 0.0 copy-start.8
  168.1 0.0 copy-start.9
  168.1 0.0 copy-start.4
  168.1 2.5 %fusion.3 = f32[2,128,1024]{2,1,0:T(8,128)} fusion(f32[2,128,1024]{2,1,0:T(8,128)S(1)} %copy-done.7, bf16[2,1024,1024]{2,1,0:T(8,128)(2,1)S(1)} %bitcast.16, pred[2]{0:T(512)(128)(4,1)S(1)} %dynamic_slice.22, s32[]{:T(128)S(6)} %select_n.37), kind=kOutput, calls=%fused_computation.8 | convolution fusion | flops 537919488 | bytes 6816260 | tf_op jit(solution)/shard_map/srk,snk->srn/dot_general | solution.py:337
  170.6 0.0 copy-done.8
  170.6 0.0 copy-done.9
  170.6 2.3 %fusion.7 = (f32[2,128,1024]{2,1,0:T(8,128)}, f32[2]{0:T(128)S(1)}, f32[2,128,1024]{2,1,0:T(8,128)}) fusion(f32[2,128,1024]{2,1,0:T(8,128)S(1)} %copy-done.8, pred[2]{0:T(512)(128)(4,1)S(1)} %dynamic_slice.22, bf16[2,1024,1024]{2,1,0:T(8,128)(2,1)S(1)} %bitcast.17, s32[]{:T(128)S(6)} %select_n.37, f32[2,128,1024]{2,1,0:T(8,128)S(1)} %copy-done.9), kind=kLoop, calls=%fused_computation.16 | loop fusion | flops 3670014 | bytes 4718606 | tf_op jit(solution)/shard_map/jit(_where)/select_n | solution.py:350
  173.0 0.1 fusion.15
  173.0 0.1 broadcast_in_dim.31.squares
  173.1 0.0 copy-done.4
  173.1 16.0 %shard_map.137 = (f32[8,128]{1,0:T(8,128)S(1)}, bf16[4,2,32,1024]{3,2,1,0:T(8,128)(2,1)S(1)}) custom-call(f32[8,128]{1,0:T(8,128)S(1)} %broadcast_in_dim.31.squares, f32[2,128,1024]{2,1,0:T(8,128)S(1)} %get-tuple-element.28.direction, f32[2,128,1024]{2,1,0:T(8,128)S(1)} %copy-done.4), custom_call_target="tpu_custom_call" | custom-call | tf_op jit(solution)/shard_map/pallas_call | solution.py:247
  189.2 0.1 multiply_reduce_fusion.2
  189.3 1.2 subtract_select_fusion
  190.5 0.7 pad_maximum_fusion
  (1 shorter events, 0.0 us)
Async XLA Ops:
  0.6 158.1 %copy-start = (bf16[2,128,1024]{2,1,0:T(8,128)(2,1)S(1)}, bf16[2,128,1024]{2,1,0:T(8,128)(2,1)}, u32[]{:S(2)}) copy-start(bf16[2,128,1024]{2,1,0:T(8,128)(2,1)} %param.13) | copy-start | bytes 1572868
  0.6 12.6 %copy-start.5 = (bf16[2,128,1024]{2,1,0:T(8,128)(2,1)S(1)}, bf16[2,128,1024]{2,1,0:T(8,128)(2,1)}, u32[]{:S(2)}) copy-start(bf16[2,128,1024]{2,1,0:T(8,128)(2,1)} %root.1) | copy-start | bytes 1572868
  154.8 1.9 %copy-start.1 = (bf16[2,4,8,32,1024]{4,3,2,1,0:T(8,128)(2,1)}, bf16[2,4,8,32,1024]{4,3,2,1,0:T(8,128)(2,1)S(1)}, u32[]{:S(2)}) copy-start(bf16[2,4,8,32,1024]{4,3,2,1,0:T(8,128)(2,1)S(1)} %get-tuple-element.10) | copy-start | bytes 12582916
  156.7 2.0 %copy-start.3 = (bf16[2,8,128,1024]{3,2,1,0:T(8,128)(2,1)}, bf16[2,8,128,1024]{3,2,1,0:T(8,128)(2,1)S(1)}, u32[]{:S(2)}) copy-start(bf16[2,8,128,1024]{3,2,1,0:T(8,128)(2,1)S(1)} %get-tuple-element.11) | copy-start | bytes 12582916
  158.7 4.9 %copy-start.6 = (f32[2,128,1024]{2,1,0:T(8,128)S(1)}, f32[2,128,1024]{2,1,0:T(8,128)}, u32[]{:S(2)}) copy-start(f32[2,128,1024]{2,1,0:T(8,128)} %param.12) | copy-start | bytes 3145732
  163.6 4.4 %copy-start.2 = (bf16[2,4,8,32,1024]{4,3,2,1,0:T(8,128)(2,1)S(1)}, bf16[2,4,8,32,1024]{4,3,2,1,0:T(8,128)(2,1)}, u32[]{:S(2)}) copy-start(bf16[2,4,8,32,1024]{4,3,2,1,0:T(8,128)(2,1)} %copy-done.1) | copy-start | bytes 12582916
  163.6 4.4 %copy-start.7 = (f32[2,128,1024]{2,1,0:T(8,128)S(1)}, f32[2,128,1024]{2,1,0:T(8,128)}, u32[]{:S(2)}) copy-start(f32[2,128,1024]{2,1,0:T(8,128)} %param.11) | copy-start | bytes 3145732
  168.1 2.6 %copy-start.8 = (f32[2,128,1024]{2,1,0:T(8,128)S(1)}, f32[2,128,1024]{2,1,0:T(8,128)}, u32[]{:S(2)}) copy-start(f32[2,128,1024]{2,1,0:T(8,128)} %param.17) | copy-start | bytes 3145732
  168.1 2.6 %copy-start.9 = (f32[2,128,1024]{2,1,0:T(8,128)S(1)}, f32[2,128,1024]{2,1,0:T(8,128)}, u32[]{:S(2)}) copy-start(f32[2,128,1024]{2,1,0:T(8,128)} %param.16) | copy-start | bytes 3145732
  168.1 5.0 %copy-start.4 = (f32[2,128,1024]{2,1,0:T(8,128)S(1)}, f32[2,128,1024]{2,1,0:T(8,128)}, u32[]{:S(2)}) copy-start(f32[2,128,1024]{2,1,0:T(8,128)} %master.1) | copy-start | bytes 3145732

commit v2 on v1

--- a/solution.py
+++ b/solution.py
@@ -106,7 +106,7 @@
 def exchange_kernel(
     dps, owns, blocks, slots, part,
     pick, grad, root, whole, roots,
-    landed, packed, p_send, p_recv, o_send, o_recv,
+    halves, sums, landed, packed, x_send, x_recv, p_send, p_recv, o_send, o_recv,
     gzs, gzr, gxs, gxr, rzs, rzr, rxs, rxr, own_sem,
 ):
     dp, own = lax.axis_index("dp"), lax.axis_index("own")
@@ -115,24 +115,42 @@
     mine.start()
     greet(dps, owns)
 
+    z, x = dp // 2, lax.rem(dp, 2)
+
+    def chunk(at):
+        return pl.ds(pl.multiple_of(at * part, part), part)
+
+    def pair(k):
+        there = lax.rem(z + k, nz)
+        rows = chunk(there * 2 + 1 - x)
+        return remote(grad.at[:, rows, :], halves.at[k], x_send.at[k], x_recv.at[k], z * 2 + 1 - x, own)
+
     def scatter(k):
-        there = lax.rem(dp + k, dps)
-        rows = pl.ds(pl.multiple_of(there * part, part), part)
-        return remote(grad.at[:, rows, :], landed.at[k - 1], p_send.at[k - 1], p_recv.at[k - 1], there, own)
-
-    for k in range(1, dps):
-        scatter(k).start()
+        there = lax.rem(z + k, nz) * 2 + x
+        return remote(sums.at[k - 1], landed.at[k - 1], p_send.at[k - 1], p_recv.at[k - 1], there, own)
+
+    order = [nz // 2] + [k for k in range(1, nz) if k != nz // 2] + [0]
+    for k in order:
+        pair(k).start()
     mine.wait()
     fetch = Gather(lambda at: roots.at[:, at], nz, (rzs, rzr, rxs, rxr))
     fetch.start()
+    for k in order[:-1]:
+        pair(k).wait_recv()
+        rows = chunk(lax.rem(z + k, nz) * 2 + x)
+        for b in range(blocks):
+            total = grad[b, rows, :].astype(jnp.float32) + halves[k, b].astype(jnp.float32)
+            sums[k - 1, b] = total.astype(jnp.bfloat16)
+        scatter(k).start()
     for t in range(nz - 2):
         fetch.step(t)
-    for k in range(1, dps):
+    pair(0).wait_recv()
+    for k in range(1, nz):
         scatter(k).wait_recv()
-    rows = pl.ds(pl.multiple_of(dp * part, part), part)
+    rows = chunk(dp)
     for b in range(blocks):
-        total = grad[b, rows, :].astype(jnp.float32)
-        for k in range(1, dps):
+        total = grad[b, rows, :].astype(jnp.float32) + halves[0, b].astype(jnp.float32)
+        for k in range(1, nz):
             total = total + landed[k - 1, b].astype(jnp.float32)
         packed[owns * slots + b] = total.astype(jnp.bfloat16)
     for s in range(owns * slots):
@@ -168,8 +186,10 @@
     spread.finish()
     for k in range(1, owns):
         deliver(k).wait_send()
-    for k in range(1, dps):
+    for k in range(1, nz):
         scatter(k).wait_send()
+    for k in range(nz):
+        pair(k).wait_send()
 
 
 def exchange(pick, grad, root, dps, owns):
@@ -187,10 +207,14 @@
         in_specs=[pl.BlockSpec(memory_space=pltpu.SMEM)] + [pl.BlockSpec(memory_space=VM)] * 2,
         out_specs=(pl.BlockSpec(memory_space=VM),) * 2,
         scratch_shapes=[
-            VM((dps - 1, blocks, part, cols), jnp.bfloat16),
+            VM((nz, blocks, part, cols), jnp.bfloat16),
+            VM((nz - 1, blocks, part, cols), jnp.bfloat16),
+            VM((nz - 1, blocks, part, cols), jnp.bfloat16),
             VM((owns * slots + blocks, part, cols), jnp.bfloat16),
-            dma((dps - 1,)),
-            dma((dps - 1,)),
+            dma((nz,)),
+            dma((nz,)),
+            dma((nz - 1,)),
+            dma((nz - 1,)),
             dma((owns - 1,)),
             dma((owns - 1,)),
         ]

time: 192 us -> 168 us (0.88)
  Pallas kernels: 158 us -> 134 us
    pallas_call x1, Pallas kernels: 142 us -> 120 us  [exchange(): pl.pallas_call(functools.partial(exchange_kernel, dps, owns, blocks, slot...]
where the time goes in v2:
time: 168 us
  Pallas kernels  134 us (80%)
  matrix products  11.9 us (7%)
  between operations  8.5 us (5%)
  other arithmetic  7.76 us (5%)
  local copies, waits for them, and re-layouts  5.59 us (3%)
    pallas_call x1, Pallas kernels, exchange(): pl.pallas_call(functools.partial(exchange_kernel, dps, owns, blocks, slot...  120 us
    pallas_call x1, Pallas kernels, finish(): pl.pallas_call(functools.partial(finish_kernel, dps, owns, slots, part),...  14.2 us
    dot_general x1, matrix products, per_device(): jnp.einsum('srk,skn->srn', mixed.astype(jnp.bfloat16), right, preferred_e...  4.93 us
    dot_general x1, matrix products, per_device(): jnp.einsum('skr,skn->srn', own_cols, whole, preferred_element_type=jnp.fl...  4.43 us
    unnamed x20, local copies, waits for them, and re-layouts  3.94 us

profile of v2, /device:TPU:1, one launch (start us, length us, event | category | flops | bytes accessed | tf_op | source)
XLA Modules:
  0.0 167.6 jit_solution(6984533143449059025)
XLA Ops:
  0.6 0.0 copy-start
  0.6 0.0 copy-start.5
  0.7 1.4 fusion.16
  9.8 0.7 fusion.12
  10.6 0.1 dynamic_slice.22
  10.6 0.1 reshape.57.pick
  10.7 2.5 %convert_bitcast_fusion.grad = bf16[4,256,1024]{2,1,0:T(8,128)(2,1)S(1)} fusion(f32[1,4,256,1024]{3,2,1,0:T(8,128)} %param.9), kind=kLoop, calls=%fused_computation | loop fusion | flops 1048576 | bytes 6291456 | tf_op jit(solution)/shard_map/convert_element_type | solution.py:327
  13.2 0.0 copy-done.5
  13.3 119.6 %shard_map.136 = (bf16[2,4,8,32,1024]{4,3,2,1,0:T(8,128)(2,1)S(1)}, bf16[2,8,128,1024]{3,2,1,0:T(8,128)(2,1)S(1)}) custom-call(f32[32]{0:T(128)S(1)} %reshape.57.pick, bf16[4,256,1024]{2,1,0:T(8,128)(2,1)S(1)} %convert_bitcast_fusion.grad, bf16[2,128,1024]{2,1,0:T(8,128)(2,1)S(1)} %copy-done.5), custom_call_target="tpu_custom_call" | custom-call | tf_op jit(solution)/shard_map/pallas_call | solution.py:201
  132.9 0.0 copy-start.1
  132.9 1.9 %copy-done.1 = bf16[2,4,8,32,1024]{4,3,2,1,0:T(8,128)(2,1)} copy-done((bf16[2,4,8,32,1024]{4,3,2,1,0:T(8,128)(2,1)}, bf16[2,4,8,32,1024]{4,3,2,1,0:T(8,128)(2,1)S(1)}, u32[]{:S(2)}) %copy-start.1) | copy-done | bytes 4194328
  134.8 0.0 copy-start.3
  134.8 2.0 %copy-done.3 = bf16[2,8,128,1024]{3,2,1,0:T(8,128)(2,1)} copy-done((bf16[2,8,128,1024]{3,2,1,0:T(8,128)(2,1)}, bf16[2,8,128,1024]{3,2,1,0:T(8,128)(2,1)S(1)}, u32[]{:S(2)}) %copy-start.3) | copy-done | bytes 4194328
  136.8 0.0 copy-done
  136.8 0.0 copy-start.6
  136.8 4.9 %multiply_reduce_fusion = (f32[2]{0:T(128)S(1)}, f32[2,128,1024]{2,1,0:T(8,128)S(1)}) fusion(bf16[2,1024,1024]{2,1,0:T(8,128)(2,1)} %bitcast.18, bf16[2,128,1024]{2,1,0:T(8,128)(2,1)S(1)} %copy-done, bf16[2,1024,1024]{2,1,0:T(8,128)(2,1)} %bitcast.14), kind=kOutput, calls=%fused_computation.14 | convolution fusion | flops 1074528256 | bytes 9961480 | tf_op jit(solution)/shard_map/srk,skn->srn/dot_general | solution.py:337
  141.7 0.0 copy-done.6
  141.7 0.0 copy-start.2
  141.8 0.0 copy-start.7
  141.8 4.4 %fusion.1 = f32[2,128,1024]{2,1,0:T(8,128)} fusion(f32[2,128,1024]{2,1,0:T(8,128)S(1)} %copy-done.6, bf16[2,1024,1024]{2,1,0:T(8,128)(2,1)} %bitcast.15, s32[]{:T(128)S(6)} %select_n.37, pred[2]{0:T(512)(128)(4,1)S(1)} %dynamic_slice.22), kind=kOutput, calls=%fused_computation.5 | convolution fusion | flops 537919488 | bytes 6815750 | tf_op jit(solution)/shard_map/skr,skn->srn/dot_general | solution.py:364
  146.2 0.0 copy-done.2
  146.2 0.0 copy-done.7
  146.2 0.0 copy-start.8
  146.2 0.0 copy-start.9
  146.2 0.0 copy-start.4
  146.2 2.5 %fusion.3 = f32[2,128,1024]{2,1,0:T(8,128)} fusion(f32[2,128,1024]{2,1,0:T(8,128)S(1)} %copy-done.7, bf16[2,1024,1024]{2,1,0:T(8,128)(2,1)S(1)} %bitcast.16, pred[2]{0:T(512)(128)(4,1)S(1)} %dynamic_slice.22, s32[]{:T(128)S(6)} %select_n.37), kind=kOutput, calls=%fused_computation.8 | convolution fusion | flops 537919488 | bytes 6816260 | tf_op jit(solution)/shard_map/srk,snk->srn/dot_general | solution.py:361
  148.8 0.0 copy-done.8
  148.8 0.0 copy-done.9
  148.8 2.3 %fusion.7 = (f32[2,128,1024]{2,1,0:T(8,128)}, f32[2]{0:T(128)S(1)}, f32[2,128,1024]{2,1,0:T(8,128)}) fusion(f32[2,128,1024]{2,1,0:T(8,128)S(1)} %copy-done.8, pred[2]{0:T(512)(128)(4,1)S(1)} %dynamic_slice.22, bf16[2,1024,1024]{2,1,0:T(8,128)(2,1)S(1)} %bitcast.17, s32[]{:T(128)S(6)} %select_n.37, f32[2,128,1024]{2,1,0:T(8,128)S(1)} %copy-done.9), kind=kLoop, calls=%fused_computation.16 | loop fusion | flops 3670014 | bytes 4718606 | tf_op jit(solution)/shard_map/jit(_where)/select_n | solution.py:374
  151.1 0.1 fusion.15
  151.2 0.1 broadcast_in_dim.31.squares
  151.3 0.0 copy-done.4
  151.3 14.2 %shard_map.137 = (f32[8,128]{1,0:T(8,128)S(1)}, bf16[4,2,32,1024]{3,2,1,0:T(8,128)(2,1)S(1)}) custom-call(f32[8,128]{1,0:T(8,128)S(1)} %broadcast_in_dim.31.squares, f32[2,128,1024]{2,1,0:T(8,128)S(1)} %get-tuple-element.28.direction, f32[2,128,1024]{2,1,0:T(8,128)S(1)} %copy-done.4), custom_call_target="tpu_custom_call" | custom-call | tf_op jit(solution)/shard_map/pallas_call | solution.py:271
  165.5 0.1 multiply_reduce_fusion.2
  165.6 1.2 subtract_select_fusion
  166.8 0.7 pad_maximum_fusion
  (1 shorter events, 0.0 us)
Async XLA Ops:
  0.6 136.2 %copy-start = (bf16[2,128,1024]{2,1,0:T(8,128)(2,1)S(1)}, bf16[2,128,1024]{2,1,0:T(8,128)(2,1)}, u32[]{:S(2)}) copy-start(bf16[2,128,1024]{2,1,0:T(8,128)(2,1)} %param.13) | copy-start | bytes 1572868
  0.6 12.6 %copy-start.5 = (bf16[2,128,1024]{2,1,0:T(8,128)(2,1)S(1)}, bf16[2,128,1024]{2,1,0:T(8,128)(2,1)}, u32[]{:S(2)}) copy-start(bf16[2,128,1024]{2,1,0:T(8,128)(2,1)} %root.1) | copy-start | bytes 1572868
  132.9 1.9 %copy-start.1 = (bf16[2,4,8,32,1024]{4,3,2,1,0:T(8,128)(2,1)}, bf16[2,4,8,32,1024]{4,3,2,1,0:T(8,128)(2,1)S(1)}, u32[]{:S(2)}) copy-start(bf16[2,4,8,32,1024]{4,3,2,1,0:T(8,128)(2,1)S(1)} %get-tuple-element.10) | copy-start | bytes 12582916
  134.8 2.0 %copy-start.3 = (bf16[2,8,128,1024]{3,2,1,0:T(8,128)(2,1)}, bf16[2,8,128,1024]{3,2,1,0:T(8,128)(2,1)S(1)}, u32[]{:S(2)}) copy-start(bf16[2,8,128,1024]{3,2,1,0:T(8,128)(2,1)S(1)} %get-tuple-element.11) | copy-start | bytes 12582916
  136.8 4.9 %copy-start.6 = (f32[2,128,1024]{2,1,0:T(8,128)S(1)}, f32[2,128,1024]{2,1,0:T(8,128)}, u32[]{:S(2)}) copy-start(f32[2,128,1024]{2,1,0:T(8,128)} %param.12) | copy-start | bytes 3145732
  141.7 4.4 %copy-start.2 = (bf16[2,4,8,32,1024]{4,3,2,1,0:T(8,128)(2,1)S(1)}, bf16[2,4,8,32,1024]{4,3,2,1,0:T(8,128)(2,1)}, u32[]{:S(2)}) copy-start(bf16[2,4,8,32,1024]{4,3,2,1,0:T(8,128)(2,1)} %copy-done.1) | copy-start | bytes 12582916
  141.8 4.4 %copy-start.7 = (f32[2,128,1024]{2,1,0:T(8,128)S(1)}, f32[2,128,1024]{2,1,0:T(8,128)}, u32[]{:S(2)}) copy-start(f32[2,128,1024]{2,1,0:T(8,128)} %param.11) | copy-start | bytes 3145732
  146.2 2.6 %copy-start.8 = (f32[2,128,1024]{2,1,0:T(8,128)S(1)}, f32[2,128,1024]{2,1,0:T(8,128)}, u32[]{:S(2)}) copy-start(f32[2,128,1024]{2,1,0:T(8,128)} %param.17) | copy-start | bytes 3145732
  146.2 2.6 %copy-start.9 = (f32[2,128,1024]{2,1,0:T(8,128)S(1)}, f32[2,128,1024]{2,1,0:T(8,128)}, u32[]{:S(2)}) copy-start(f32[2,128,1024]{2,1,0:T(8,128)} %param.16) | copy-start | bytes 3145732
  146.2 5.0 %copy-start.4 = (f32[2,128,1024]{2,1,0:T(8,128)S(1)}, f32[2,128,1024]{2,1,0:T(8,128)}, u32[]{:S(2)}) copy-start(f32[2,128,1024]{2,1,0:T(8,128)} %master.1) | copy-start | bytes 3145732

commit v3 on v2

--- a/solution.py
+++ b/solution.py
@@ -38,9 +38,9 @@
 
 
 class Gather:
-    def __init__(self, piece, nz, sems):
-        self.piece, self.nz = piece, nz
-        self.zs, self.zr, self.xs, self.xr = sems
+    def __init__(self, piece, main, side, nz, sems):
+        self.piece, self.main, self.side, self.nz = piece, main, side, nz
+        self.zs, self.zr, self.xs, self.xr, self.ss, self.sr = sems
         dp = lax.axis_index("dp")
         self.own = lax.axis_index("own")
         self.z, self.x = dp // 2, lax.rem(dp, 2)
@@ -57,7 +57,7 @@
         sign = 1 - 2 * way
         at = self.z - sign * t
         ok = (at >= 0) & (at < self.nz)
-        ref = self.piece(at * 2 + self.x)
+        ref = (self.main if t else self.piece)(at * 2 + self.x)
         return ok, remote(ref, ref, self.xs.at[way, t], self.xr.at[way, t], self.z * 2 + 1 - self.x, self.own)
 
     def came(self, way, t):
@@ -71,8 +71,23 @@
         sign = 1 - 2 * way
         at = self.z - sign * t
         ok = (at >= 0) & (at < self.nz)
-        ref = self.piece(at * 2 + 1 - self.x)
+        ref = (self.main if t else self.piece)(at * 2 + 1 - self.x)
         return ok, remote(ref, ref, self.xs.at[way, t], self.xr.at[way, t], self.z * 2 + 1 - self.x, self.own)
+
+    def aside(self, way, t):
+        sign = 1 - 2 * way
+        at = self.z - sign * t
+        there = self.z + sign
+        ok = (at >= 0) & (at < self.nz) & (there >= 0) & (there < self.nz)
+        ref = self.side(at * 2 + 1 - self.x)
+        return ok, remote(ref, ref, self.ss.at[way, t], self.sr.at[way, t], there * 2 + self.x, self.own)
+
+    def joined(self, way, t):
+        sign = 1 - 2 * way
+        at = self.z - sign * (t + 1)
+        ok = (at >= 0) & (at < self.nz)
+        ref = self.side(at * 2 + 1 - self.x)
+        return ok, remote(ref, ref, self.ss.at[way, t], self.sr.at[way, t], self.z * 2 + 1 - self.x, self.own)
 
     def start(self):
         for way in range(2):
@@ -81,6 +96,11 @@
         self.across(0, 0)[1].start()
 
     def step(self, t):
+        if t == 0:
+            self.crossed(0, 0)[1].wait_recv()
+            for way in range(2):
+                ok, copy = self.aside(way, 0)
+                pl.when(ok)(copy.start)
         for way in range(2):
             ok, copy = self.came(way, t)
             pl.when(ok)(copy.wait_recv)
@@ -89,25 +109,39 @@
                 pl.when(ok)(copy.start)
             ok, copy = self.across(way, t + 1)
             pl.when(ok)(copy.start)
+            if t > 0:
+                self.joining(way, t - 1)
+
+    def joining(self, way, t):
+        ok, copy = self.joined(way, t)
+        pl.when(ok)(copy.wait_recv)
+        if t + 1 < self.nz - 1:
+            ok, copy = self.aside(way, t + 1)
+            pl.when(ok)(copy.start)
 
     def finish(self):
+        for way in range(2):
+            self.joining(way, self.nz - 2)
         for t in range(self.nz):
             for way in range(1 if t == 0 else 2):
-                ok, copy = self.crossed(way, t)
-                pl.when(ok)(copy.wait_recv)
+                if t > 0:
+                    ok, copy = self.crossed(way, t)
+                    pl.when(ok)(copy.wait_recv)
                 ok, copy = self.across(way, t)
                 pl.when(ok)(copy.wait_send)
         for t in range(self.nz - 1):
             for way in range(2):
                 ok, copy = self.along(way, t)
                 pl.when(ok)(copy.wait_send)
+                ok, copy = self.aside(way, t)
+                pl.when(ok)(copy.wait_send)
 
 
 def exchange_kernel(
     dps, owns, blocks, slots, part,
     pick, grad, root, whole, roots,
     halves, sums, landed, packed, x_send, x_recv, p_send, p_recv, o_send, o_recv,
-    gzs, gzr, gxs, gxr, rzs, rzr, rxs, rxr, own_sem,
+    gzs, gzr, gxs, gxr, gss, gsr, rzs, rzr, rxs, rxr, rss, rsr, own_sem,
 ):
     dp, own = lax.axis_index("dp"), lax.axis_index("own")
     nz = dps // 2
@@ -133,7 +167,15 @@
     for k in order:
         pair(k).start()
     mine.wait()
-    fetch = Gather(lambda at: roots.at[:, at], nz, (rzs, rzr, rxs, rxr))
+    height = root.shape[1]
+    quarter = height // 4
+    fetch = Gather(
+        lambda at: roots.at[:, at],
+        lambda at: roots.at[:, at, pl.ds(quarter, height - quarter)],
+        lambda at: roots.at[:, at, pl.ds(0, quarter)],
+        nz,
+        (rzs, rzr, rxs, rxr, rss, rsr),
+    )
     fetch.start()
     for k in order[:-1]:
         pair(k).wait_recv()
@@ -178,7 +220,13 @@
     fetch.step(nz - 2)
     for k in range(1, owns):
         delivered(k).wait_recv()
-    spread = Gather(lambda at: whole.at[:, :, at], nz, (gzs, gzr, gxs, gxr))
+    spread = Gather(
+        lambda at: whole.at[:, :, at],
+        lambda at: whole.at[:, pl.ds(1, owns - 1), at],
+        lambda at: whole.at[:, 0, at],
+        nz,
+        (gzs, gzr, gxs, gxr, gss, gsr),
+    )
     spread.start()
     for t in range(nz - 1):
         spread.step(t)
@@ -218,7 +266,7 @@
             dma((owns - 1,)),
             dma((owns - 1,)),
         ]
-        + [dma((2, nz))] * 8
+        + [dma((2, nz))] * 12
         + [dma],
         compiler_params=pltpu.CompilerParams(collective_id=0, has_side_effects=True, vmem_limit_bytes=40 * MIB),
     )(pick, grad, root)
@@ -321,7 +369,7 @@
     owned_slots = owners * slot_count
     matches = owner_map[:, None] == jnp.arange(owned_slots, dtype=jnp.int32)[None, :]
     occupied = jnp.any(matches, axis=0)
-    kernels = groups % 2 == 0 and (grads.shape[2] // groups) % 16 == 0 and (rows_dev // owners) % 16 == 0
+    kernels = groups % 2 == 0 and (grads.shape[2] // groups) % 16 == 0 and (rows_dev // owners) % 16 == 0 and rows_dev % 64 == 0
     if kernels:
         pick = matches.astype(jnp.float32).reshape(-1)
         whole, right = exchange(pick, grads[0].astype(jnp.bfloat16), root_right, groups, owners)
@@ -372,9 +420,9 @@
     master_next = jnp.where(occupied_mine, master_new, master)
     first_next = jnp.where(occupied_mine, first_new, moment_first)
     second_next = jnp.where(occupied_mine, second_new, moment_second)
-    weights_out = jnp.stack(
-        [lax.dynamic_index_in_dim(delivered, owner_map[b], 0, keepdims=False) for b in range(blocks)]
-    )
+    weights_out = jnp.zeros((blocks,) + delivered.shape[1:], delivered.dtype)
+    for s in range(owned_slots):
+        weights_out = jnp.where(matches[:, s, None, None], delivered[s][None], weights_out)
     return (left_next, right_next, master_next, first_next, second_next, weights_out)
 
 

time: 168 us -> 157 us (0.935)
  between operations: 8.5 us -> 0.74 us
  Pallas kernels: 134 us -> 132 us
    pallas_call x1, Pallas kernels: 120 us -> 115 us  [exchange(): pl.pallas_call(functools.partial(exchange_kernel, dps, owns, blocks, slot...]
    pallas_call x1, Pallas kernels: 14.2 us -> 17.1 us  [finish(): pl.pallas_call(functools.partial(finish_kernel, dps, owns, slots, part),...]
where the time goes in v3:
time: 157 us
  Pallas kernels  132 us (84%)
  matrix products  11.9 us (8%)
  other arithmetic  8.03 us (5%)
  local copies, waits for them, and re-layouts  4.3 us (3%)
    pallas_call x1, Pallas kernels, exchange(): pl.pallas_call(functools.partial(exchange_kernel, dps, owns, blocks, slot...  115 us
    pallas_call x1, Pallas kernels, finish(): pl.pallas_call(functools.partial(finish_kernel, dps, owns, slots, part),...  17.1 us
    dot_general x1, matrix products, per_device(): jnp.einsum('srk,skn->srn', mixed.astype(jnp.bfloat16), right, preferred_e...  4.93 us
    dot_general x1, matrix products, per_device(): jnp.einsum('skr,skn->srn', own_cols, whole, preferred_element_type=jnp.fl...  4.43 us
    unnamed x20, local copies, waits for them, and re-layouts  3.94 us

profile of v3, /device:TPU:1, one launch (start us, length us, event | category | flops | bytes accessed | tf_op | source)
XLA Modules:
  0.0 156.9 jit_solution(4538792996602110911)
XLA Ops:
  0.6 0.0 copy-start
  0.6 0.0 copy-start.5
  0.7 0.9 iota_compare_fusion
  1.5 0.1 dynamic_slice.9
  1.6 0.1 copy.17
  1.7 0.1 reshape.65.pick
  1.8 2.5 %convert_bitcast_fusion.grad = bf16[4,256,1024]{2,1,0:T(8,128)(2,1)S(1)} fusion(f32[1,4,256,1024]{3,2,1,0:T(8,128)} %param.9), kind=kLoop, calls=%fused_computation | loop fusion | flops 1048576 | bytes 6291456 | tf_op jit(solution)/shard_map/convert_element_type | solution.py:375
  4.3 0.0 copy-done.5
  4.3 114.8 %shard_map.136 = (bf16[2,4,8,32,1024]{4,3,2,1,0:T(8,128)(2,1)S(1)}, bf16[2,8,128,1024]{3,2,1,0:T(8,128)(2,1)S(1)}) custom-call(f32[32]{0:T(128)S(1)} %reshape.65.pick, bf16[4,256,1024]{2,1,0:T(8,128)(2,1)S(1)} %convert_bitcast_fusion.grad, bf16[2,128,1024]{2,1,0:T(8,128)(2,1)S(1)} %copy-done.5), custom_call_target="tpu_custom_call" | custom-call | tf_op jit(solution)/shard_map/pallas_call | solution.py:249
  119.2 0.0 copy-start.1
  119.2 1.9 %copy-done.1 = bf16[2,4,8,32,1024]{4,3,2,1,0:T(8,128)(2,1)} copy-done((bf16[2,4,8,32,1024]{4,3,2,1,0:T(8,128)(2,1)}, bf16[2,4,8,32,1024]{4,3,2,1,0:T(8,128)(2,1)S(1)}, u32[]{:S(2)}) %copy-start.1) | copy-done | bytes 4194328
  121.1 0.0 copy-start.3
  121.1 2.0 %copy-done.3 = bf16[2,8,128,1024]{3,2,1,0:T(8,128)(2,1)} copy-done((bf16[2,8,128,1024]{3,2,1,0:T(8,128)(2,1)}, bf16[2,8,128,1024]{3,2,1,0:T(8,128)(2,1)S(1)}, u32[]{:S(2)}) %copy-start.3) | copy-done | bytes 4194328
  123.1 0.0 copy-done
  123.1 0.0 copy-start.6
  123.1 4.9 %multiply_reduce_fusion = (f32[2]{0:T(128)S(1)}, f32[2,128,1024]{2,1,0:T(8,128)S(1)}) fusion(bf16[2,1024,1024]{2,1,0:T(8,128)(2,1)} %bitcast.46, bf16[2,128,1024]{2,1,0:T(8,128)(2,1)S(1)} %copy-done, bf16[2,1024,1024]{2,1,0:T(8,128)(2,1)} %bitcast.42), kind=kOutput, calls=%fused_computation.14 | convolution fusion | flops 1074528256 | bytes 9961480 | tf_op jit(solution)/shard_map/srk,skn->srn/dot_general | solution.py:385
  128.0 0.0 copy-done.6
  128.0 0.0 copy-start.2
  128.0 0.0 copy-start.7
  128.0 4.4 %fusion.1 = f32[2,128,1024]{2,1,0:T(8,128)} fusion(f32[2,128,1024]{2,1,0:T(8,128)S(1)} %copy-done.6, bf16[2,1024,1024]{2,1,0:T(8,128)(2,1)} %bitcast.43, s32[]{:T(128)S(6)} %select_n.49, pred[2]{0:T(512)(128)(4,1)S(1)} %dynamic_slice.9), kind=kOutput, calls=%fused_computation.5 | convolution fusion | flops 537919488 | bytes 6815750 | tf_op jit(solution)/shard_map/skr,skn->srn/dot_general | solution.py:412
  132.4 0.0 copy-done.2
  132.4 0.0 copy-done.7
  132.4 0.0 copy-start.8
  132.5 0.0 copy-start.9
  132.5 0.0 copy-start.4
  132.5 2.5 %fusion.3 = f32[2,128,1024]{2,1,0:T(8,128)} fusion(f32[2,128,1024]{2,1,0:T(8,128)S(1)} %copy-done.7, bf16[2,1024,1024]{2,1,0:T(8,128)(2,1)S(1)} %bitcast.44, pred[2]{0:T(512)(128)(4,1)S(1)} %dynamic_slice.9, s32[]{:T(128)S(6)} %select_n.49), kind=kOutput, calls=%fused_computation.8 | convolution fusion | flops 537919488 | bytes 6816260 | tf_op jit(solution)/shard_map/srk,snk->srn/dot_general | solution.py:409
  135.0 0.0 copy-done.8
  135.0 0.0 copy-done.9
  135.0 2.3 %fusion.7 = (f32[2,128,1024]{2,1,0:T(8,128)}, f32[2]{0:T(128)S(1)}, f32[2,128,1024]{2,1,0:T(8,128)}) fusion(f32[2,128,1024]{2,1,0:T(8,128)S(1)} %copy-done.8, pred[2]{0:T(512)(128)(4,1)S(1)} %dynamic_slice.9, bf16[2,1024,1024]{2,1,0:T(8,128)(2,1)S(1)} %bitcast.45, s32[]{:T(128)S(6)} %select_n.49, f32[2,128,1024]{2,1,0:T(8,128)S(1)} %copy-done.9), kind=kLoop, calls=%fused_computation.16 | loop fusion | flops 3670014 | bytes 4718606 | tf_op jit(solution)/shard_map/jit(_where)/select_n | solution.py:422
  137.4 0.1 fusion.13
  137.4 0.1 broadcast_in_dim.152.squares
  137.5 0.0 copy-done.4
  137.5 17.1 %shard_map.137 = (f32[8,128]{1,0:T(8,128)S(1)}, bf16[4,2,32,1024]{3,2,1,0:T(8,128)(2,1)S(1)}) custom-call(f32[8,128]{1,0:T(8,128)S(1)} %broadcast_in_dim.152.squares, f32[2,128,1024]{2,1,0:T(8,128)S(1)} %get-tuple-element.37.direction, f32[2,128,1024]{2,1,0:T(8,128)S(1)} %copy-done.4), custom_call_target="tpu_custom_call" | custom-call | tf_op jit(solution)/shard_map/pallas_call | solution.py:319
  154.6 0.1 multiply_reduce_fusion.2
  154.8 1.2 subtract_select_fusion
  156.0 0.9 select_select_fusion
  (2 shorter events, 0.0 us)
Async XLA Ops:
  0.6 122.4 %copy-start = (bf16[2,128,1024]{2,1,0:T(8,128)(2,1)S(1)}, bf16[2,128,1024]{2,1,0:T(8,128)(2,1)}, u32[]{:S(2)}) copy-start(bf16[2,128,1024]{2,1,0:T(8,128)(2,1)} %param.13) | copy-start | bytes 1572868
  0.6 3.7 %copy-start.5 = (bf16[2,128,1024]{2,1,0:T(8,128)(2,1)S(1)}, bf16[2,128,1024]{2,1,0:T(8,128)(2,1)}, u32[]{:S(2)}) copy-start(bf16[2,128,1024]{2,1,0:T(8,128)(2,1)} %root.1) | copy-start | bytes 1572868
  119.2 1.9 %copy-start.1 = (bf16[2,4,8,32,1024]{4,3,2,1,0:T(8,128)(2,1)}, bf16[2,4,8,32,1024]{4,3,2,1,0:T(8,128)(2,1)S(1)}, u32[]{:S(2)}) copy-start(bf16[2,4,8,32,1024]{4,3,2,1,0:T(8,128)(2,1)S(1)} %get-tuple-element.10) | copy-start | bytes 12582916
  121.1 2.0 %copy-start.3 = (bf16[2,8,128,1024]{3,2,1,0:T(8,128)(2,1)}, bf16[2,8,128,1024]{3,2,1,0:T(8,128)(2,1)S(1)}, u32[]{:S(2)}) copy-start(bf16[2,8,128,1024]{3,2,1,0:T(8,128)(2,1)S(1)} %get-tuple-element.11) | copy-start | bytes 12582916
  123.1 4.9 %copy-start.6 = (f32[2,128,1024]{2,1,0:T(8,128)S(1)}, f32[2,128,1024]{2,1,0:T(8,128)}, u32[]{:S(2)}) copy-start(f32[2,128,1024]{2,1,0:T(8,128)} %param.12) | copy-start | bytes 3145732
  128.0 4.4 %copy-start.2 = (bf16[2,4,8,32,1024]{4,3,2,1,0:T(8,128)(2,1)S(1)}, bf16[2,4,8,32,1024]{4,3,2,1,0:T(8,128)(2,1)}, u32[]{:S(2)}) copy-start(bf16[2,4,8,32,1024]{4,3,2,1,0:T(8,128)(2,1)} %copy-done.1) | copy-start | bytes 12582916
  128.0 4.4 %copy-start.7 = (f32[2,128,1024]{2,1,0:T(8,128)S(1)}, f32[2,128,1024]{2,1,0:T(8,128)}, u32[]{:S(2)}) copy-start(f32[2,128,1024]{2,1,0:T(8,128)} %param.11) | copy-start | bytes 3145732
  132.4 2.6 %copy-start.8 = (f32[2,128,1024]{2,1,0:T(8,128)S(1)}, f32[2,128,1024]{2,1,0:T(8,128)}, u32[]{:S(2)}) copy-start(f32[2,128,1024]{2,1,0:T(8,128)} %param.17) | copy-start | bytes 3145732
  132.5 2.6 %copy-start.9 = (f32[2,128,1024]{2,1,0:T(8,128)S(1)}, f32[2,128,1024]{2,1,0:T(8,128)}, u32[]{:S(2)}) copy-start(f32[2,128,1024]{2,1,0:T(8,128)} %param.16) | copy-start | bytes 3145732
  132.5 5.0 %copy-start.4 = (f32[2,128,1024]{2,1,0:T(8,128)S(1)}, f32[2,128,1024]{2,1,0:T(8,128)}, u32[]{:S(2)}) copy-start(f32[2,128,1024]{2,1,0:T(8,128)} %master.1) | copy-start | bytes 3145732

commit v4 on v3

--- a/solution.py
+++ b/solution.py
@@ -215,9 +215,10 @@
 
     for k in range(1, owns):
         deliver(k).start()
-    for s in range(slots):
-        whole[s, own, dp] = packed[own * slots + s]
+    kept = pltpu.make_async_copy(packed.at[pl.ds(own * slots, slots)], whole.at[:, own, dp], own_sem)
+    kept.start()
     fetch.step(nz - 2)
+    kept.wait()
     for k in range(1, owns):
         delivered(k).wait_recv()
     spread = Gather(
@@ -253,7 +254,7 @@
             jax.ShapeDtypeStruct((slots, dps, rows_dev, cols), jnp.bfloat16),
         ),
         in_specs=[pl.BlockSpec(memory_space=pltpu.SMEM)] + [pl.BlockSpec(memory_space=VM)] * 2,
-        out_specs=(pl.BlockSpec(memory_space=VM),) * 2,
+        out_specs=(pl.BlockSpec(memory_space=pltpu.HBM),) * 2,
         scratch_shapes=[
             VM((nz, blocks, part, cols), jnp.bfloat16),
             VM((nz - 1, blocks, part, cols), jnp.bfloat16),
@@ -268,7 +269,7 @@
         ]
         + [dma((2, nz))] * 12
         + [dma],
-        compiler_params=pltpu.CompilerParams(collective_id=0, has_side_effects=True, vmem_limit_bytes=40 * MIB),
+        compiler_params=pltpu.CompilerParams(collective_id=0, has_side_effects=True, vmem_limit_bytes=56 * MIB),
     )(pick, grad, root)
 
 

time: 157 us -> 157 us (level)
  local copies, waits for them, and re-layouts: 4.3 us -> 0.91 us
  Pallas kernels: 132 us -> 134 us
    unnamed x20 -> x14, local copies, waits for them, and re-layouts: 3.94 us -> 0.04 us
    pallas_call x1, Pallas kernels: 115 us -> 117 us  [exchange(): pl.pallas_call(functools.partial(exchange_kernel, dps, owns, blocks, slot...]
where the time goes in v4:
time: 157 us
  Pallas kernels  134 us (85%)
  matrix products  11.9 us (8%)
  other arithmetic  9.38 us (6%)
    pallas_call x1, Pallas kernels, exchange(): pl.pallas_call(functools.partial(exchange_kernel, dps, owns, blocks, slot...  117 us
    pallas_call x1, Pallas kernels, finish(): pl.pallas_call(functools.partial(finish_kernel, dps, owns, slots, part),...  16.8 us
    dot_general x1, matrix products, per_device(): jnp.einsum('srk,skn->srn', mixed.astype(jnp.bfloat16), right, preferred_e...  4.93 us
    dot_general x1, matrix products, per_device(): jnp.einsum('skr,skn->srn', own_cols, whole, preferred_element_type=jnp.fl...  4.43 us
    convert_element_type x1, other arithmetic, per_device(): grads[0].astype(jnp.bfloat16)  3.89 us

profile of v4, /device:TPU:1, one launch (start us, length us, event | category | flops | bytes accessed | tf_op | source)
XLA Modules:
  0.0 156.7 jit_solution(7714228652924732121)
XLA Ops:
  0.6 0.0 copy-start
  0.7 0.8 iota_compare_fusion
  1.5 0.1 dynamic_slice.9
  1.6 0.1 copy.17
  1.6 0.6 reshape.65.pick
  2.3 3.9 %convert_bitcast_fusion.grad = bf16[4,256,1024]{2,1,0:T(8,128)(2,1)} fusion(f32[1,4,256,1024]{3,2,1,0:T(8,128)} %param.9), kind=kLoop, calls=%fused_computation | loop fusion | flops 1048576 | bytes 6291456 | tf_op jit(solution)/shard_map/convert_element_type | solution.py:376
  6.1 117.0 %shard_map.136 = (bf16[2,4,8,32,1024]{4,3,2,1,0:T(8,128)(2,1)}, bf16[2,8,128,1024]{3,2,1,0:T(8,128)(2,1)}) custom-call(f32[32]{0:T(128)} %reshape.65.pick, bf16[4,256,1024]{2,1,0:T(8,128)(2,1)} %convert_bitcast_fusion.grad, bf16[2,128,1024]{2,1,0:T(8,128)(2,1)} %root.1), custom_call_target="tpu_custom_call" | custom-call | tf_op jit(solution)/shard_map/pallas_call | solution.py:250
  123.1 0.0 copy-done
  123.1 0.0 copy-start.3
  123.1 4.9 %multiply_reduce_fusion = (f32[2]{0:T(128)S(1)}, f32[2,128,1024]{2,1,0:T(8,128)S(1)}) fusion(bf16[2,1024,1024]{2,1,0:T(8,128)(2,1)} %bitcast.47, bf16[2,128,1024]{2,1,0:T(8,128)(2,1)S(1)} %copy-done, bf16[2,1024,1024]{2,1,0:T(8,128)(2,1)} %bitcast.43), kind=kOutput, calls=%fused_computation.14 | convolution fusion | flops 1074528256 | bytes 9961480 | tf_op jit(solution)/shard_map/srk,skn->srn/dot_general | solution.py:386
  128.1 0.0 copy-done.3
  128.1 0.0 copy-start.2
  128.1 0.0 copy-start.4
  128.1 4.4 %fusion.1 = f32[2,128,1024]{2,1,0:T(8,128)} fusion(f32[2,128,1024]{2,1,0:T(8,128)S(1)} %copy-done.3, bf16[2,1024,1024]{2,1,0:T(8,128)(2,1)} %bitcast.44, s32[]{:T(128)S(6)} %select_n.49, pred[2]{0:T(512)(128)(4,1)S(1)} %dynamic_slice.9), kind=kOutput, calls=%fused_computation.5 | convolution fusion | flops 537919488 | bytes 6815750 | tf_op jit(solution)/shard_map/skr,skn->srn/dot_general | solution.py:413
  132.5 0.0 copy-done.2
  132.5 0.0 copy-done.4
  132.5 0.0 copy-start.5
  132.5 0.0 copy-start.6
  132.5 0.0 copy-start.1
  132.6 2.5 %fusion.3 = f32[2,128,1024]{2,1,0:T(8,128)} fusion(f32[2,128,1024]{2,1,0:T(8,128)S(1)} %copy-done.4, bf16[2,1024,1024]{2,1,0:T(8,128)(2,1)S(1)} %bitcast.45, pred[2]{0:T(512)(128)(4,1)S(1)} %dynamic_slice.9, s32[]{:T(128)S(6)} %select_n.49), kind=kOutput, calls=%fused_computation.8 | convolution fusion | flops 537919488 | bytes 6816260 | tf_op jit(solution)/shard_map/srk,snk->srn/dot_general | solution.py:410
  135.1 0.0 copy-done.5
  135.1 0.0 copy-done.6
  135.1 2.3 %fusion.7 = (f32[2,128,1024]{2,1,0:T(8,128)}, f32[2]{0:T(128)S(1)}, f32[2,128,1024]{2,1,0:T(8,128)}) fusion(f32[2,128,1024]{2,1,0:T(8,128)S(1)} %copy-done.5, pred[2]{0:T(512)(128)(4,1)S(1)} %dynamic_slice.9, bf16[2,1024,1024]{2,1,0:T(8,128)(2,1)S(1)} %bitcast.46, s32[]{:T(128)S(6)} %select_n.49, f32[2,128,1024]{2,1,0:T(8,128)S(1)} %copy-done.6), kind=kLoop, calls=%fused_computation.16 | loop fusion | flops 3670014 | bytes 4718606 | tf_op jit(solution)/shard_map/jit(_where)/select_n | solution.py:423
  137.4 0.1 fusion.13
  137.5 0.1 broadcast_in_dim.152.squares
  137.6 0.0 copy-done.1
  137.6 16.8 %shard_map.137 = (f32[8,128]{1,0:T(8,128)S(1)}, bf16[4,2,32,1024]{3,2,1,0:T(8,128)(2,1)S(1)}) custom-call(f32[8,128]{1,0:T(8,128)S(1)} %broadcast_in_dim.152.squares, f32[2,128,1024]{2,1,0:T(8,128)S(1)} %get-tuple-element.37.direction, f32[2,128,1024]{2,1,0:T(8,128)S(1)} %copy-done.1), custom_call_target="tpu_custom_call" | custom-call | tf_op jit(solution)/shard_map/pallas_call | solution.py:320
  154.4 0.1 multiply_reduce_fusion.2
  154.5 1.2 subtract_select_fusion
  155.8 0.9 select_select_fusion
  (2 shorter events, 0.0 us)
Async XLA Ops:
  0.6 122.5 %copy-start = (bf16[2,128,1024]{2,1,0:T(8,128)(2,1)S(1)}, bf16[2,128,1024]{2,1,0:T(8,128)(2,1)}, u32[]{:S(2)}) copy-start(bf16[2,128,1024]{2,1,0:T(8,128)(2,1)} %param.13) | copy-start | bytes 1572868
  123.1 4.9 %copy-start.3 = (f32[2,128,1024]{2,1,0:T(8,128)S(1)}, f32[2,128,1024]{2,1,0:T(8,128)}, u32[]{:S(2)}) copy-start(f32[2,128,1024]{2,1,0:T(8,128)} %param.12) | copy-start | bytes 3145732
  128.1 4.4 %copy-start.2 = (bf16[2,4,8,32,1024]{4,3,2,1,0:T(8,128)(2,1)S(1)}, bf16[2,4,8,32,1024]{4,3,2,1,0:T(8,128)(2,1)}, u32[]{:S(2)}) copy-start(bf16[2,4,8,32,1024]{4,3,2,1,0:T(8,128)(2,1)} %get-tuple-element.10) | copy-start | bytes 12582916
  128.1 4.4 %copy-start.4 = (f32[2,128,1024]{2,1,0:T(8,128)S(1)}, f32[2,128,1024]{2,1,0:T(8,128)}, u32[]{:S(2)}) copy-start(f32[2,128,1024]{2,1,0:T(8,128)} %param.11) | copy-start | bytes 3145732
  132.5 2.6 %copy-start.5 = (f32[2,128,1024]{2,1,0:T(8,128)S(1)}, f32[2,128,1024]{2,1,0:T(8,128)}, u32[]{:S(2)}) copy-start(f32[2,128,1024]{2,1,0:T(8,128)} %param.17) | copy-start | bytes 3145732
  132.5 2.6 %copy-start.6 = (f32[2,128,1024]{2,1,0:T(8,128)S(1)}, f32[2,128,1024]{2,1,0:T(8,128)}, u32[]{:S(2)}) copy-start(f32[2,128,1024]{2,1,0:T(8,128)} %param.16) | copy-start | bytes 3145732
  132.5 5.0 %copy-start.1 = (f32[2,128,1024]{2,1,0:T(8,128)S(1)}, f32[2,128,1024]{2,1,0:T(8,128)}, u32[]{:S(2)}) copy-start(f32[2,128,1024]{2,1,0:T(8,128)} %master.1) | copy-start | bytes 3145732

commit v5 on v4

--- a/solution.py
+++ b/solution.py
@@ -184,8 +184,7 @@
             total = grad[b, rows, :].astype(jnp.float32) + halves[k, b].astype(jnp.float32)
             sums[k - 1, b] = total.astype(jnp.bfloat16)
         scatter(k).start()
-    for t in range(nz - 2):
-        fetch.step(t)
+    fetch.step(0)
     pair(0).wait_recv()
     for k in range(1, nz):
         scatter(k).wait_recv()
@@ -217,7 +216,6 @@
         deliver(k).start()
     kept = pltpu.make_async_copy(packed.at[pl.ds(own * slots, slots)], whole.at[:, own, dp], own_sem)
     kept.start()
-    fetch.step(nz - 2)
     kept.wait()
     for k in range(1, owns):
         delivered(k).wait_recv()
@@ -230,6 +228,8 @@
     )
     spread.start()
     for t in range(nz - 1):
+        if t > 0:
+            fetch.step(t)
         spread.step(t)
     fetch.finish()
     spread.finish()

time: 157 us -> 157 us (level)
  no operation moved by 1% of the time
where the time goes in v5:
time: 157 us
  Pallas kernels  134 us (85%)
  matrix products  11.9 us (8%)
  other arithmetic  9.38 us (6%)
    pallas_call x1, Pallas kernels, exchange(): pl.pallas_call(functools.partial(exchange_kernel, dps, owns, blocks, slot...  118 us
    pallas_call x1, Pallas kernels, finish(): pl.pallas_call(functools.partial(finish_kernel, dps, owns, slots, part),...  15.3 us
    dot_general x1, matrix products, per_device(): jnp.einsum('srk,skn->srn', mixed.astype(jnp.bfloat16), right, preferred_e...  4.93 us
    dot_general x1, matrix products, per_device(): jnp.einsum('skr,skn->srn', own_cols, whole, preferred_element_type=jnp.fl...  4.43 us
    convert_element_type x1, other arithmetic, per_device(): grads[0].astype(jnp.bfloat16)  3.89 us

profile of v5, /device:TPU:1, one launch (start us, length us, event | category | flops | bytes accessed | tf_op | source)
XLA Modules:
  0.0 156.5 jit_solution(9745750191052746573)
XLA Ops:
  0.6 0.0 copy-start
  0.7 0.8 iota_compare_fusion
  1.5 0.1 dynamic_slice.9
  1.6 0.1 copy.17
  1.6 0.6 reshape.65.pick
  2.3 3.9 %convert_bitcast_fusion.grad = bf16[4,256,1024]{2,1,0:T(8,128)(2,1)} fusion(f32[1,4,256,1024]{3,2,1,0:T(8,128)} %param.9), kind=kLoop, calls=%fused_computation | loop fusion | flops 1048576 | bytes 6291456 | tf_op jit(solution)/shard_map/convert_element_type | solution.py:376
  6.1 118.3 %shard_map.136 = (bf16[2,4,8,32,1024]{4,3,2,1,0:T(8,128)(2,1)}, bf16[2,8,128,1024]{3,2,1,0:T(8,128)(2,1)}) custom-call(f32[32]{0:T(128)} %reshape.65.pick, bf16[4,256,1024]{2,1,0:T(8,128)(2,1)} %convert_bitcast_fusion.grad, bf16[2,128,1024]{2,1,0:T(8,128)(2,1)} %root.1), custom_call_target="tpu_custom_call" | custom-call | tf_op jit(solution)/shard_map/pallas_call | solution.py:250
  124.5 0.0 copy-done
  124.5 0.0 copy-start.3
  124.5 4.9 %multiply_reduce_fusion = (f32[2]{0:T(128)S(1)}, f32[2,128,1024]{2,1,0:T(8,128)S(1)}) fusion(bf16[2,1024,1024]{2,1,0:T(8,128)(2,1)} %bitcast.47, bf16[2,128,1024]{2,1,0:T(8,128)(2,1)S(1)} %copy-done, bf16[2,1024,1024]{2,1,0:T(8,128)(2,1)} %bitcast.43), kind=kOutput, calls=%fused_computation.14 | convolution fusion | flops 1074528256 | bytes 9961480 | tf_op jit(solution)/shard_map/srk,skn->srn/dot_general | solution.py:386
  129.4 0.0 copy-done.3
  129.4 0.0 copy-start.2
  129.4 0.0 copy-start.4
  129.5 4.4 %fusion.1 = f32[2,128,1024]{2,1,0:T(8,128)} fusion(f32[2,128,1024]{2,1,0:T(8,128)S(1)} %copy-done.3, bf16[2,1024,1024]{2,1,0:T(8,128)(2,1)} %bitcast.44, s32[]{:T(128)S(6)} %select_n.49, pred[2]{0:T(512)(128)(4,1)S(1)} %dynamic_slice.9), kind=kOutput, calls=%fused_computation.5 | convolution fusion | flops 537919488 | bytes 6815750 | tf_op jit(solution)/shard_map/skr,skn->srn/dot_general | solution.py:413
  133.9 0.0 copy-done.2
  133.9 0.0 copy-done.4
  133.9 0.0 copy-start.5
  133.9 0.0 copy-start.6
  133.9 0.0 copy-start.1
  133.9 2.5 %fusion.3 = f32[2,128,1024]{2,1,0:T(8,128)} fusion(f32[2,128,1024]{2,1,0:T(8,128)S(1)} %copy-done.4, bf16[2,1024,1024]{2,1,0:T(8,128)(2,1)S(1)} %bitcast.45, pred[2]{0:T(512)(128)(4,1)S(1)} %dynamic_slice.9, s32[]{:T(128)S(6)} %select_n.49), kind=kOutput, calls=%fused_computation.8 | convolution fusion | flops 537919488 | bytes 6816260 | tf_op jit(solution)/shard_map/srk,snk->srn/dot_general | solution.py:410
  136.4 0.0 copy-done.5
  136.4 0.0 copy-done.6
  136.4 2.3 %fusion.7 = (f32[2,128,1024]{2,1,0:T(8,128)}, f32[2]{0:T(128)S(1)}, f32[2,128,1024]{2,1,0:T(8,128)}) fusion(f32[2,128,1024]{2,1,0:T(8,128)S(1)} %copy-done.5, pred[2]{0:T(512)(128)(4,1)S(1)} %dynamic_slice.9, bf16[2,1024,1024]{2,1,0:T(8,128)(2,1)S(1)} %bitcast.46, s32[]{:T(128)S(6)} %select_n.49, f32[2,128,1024]{2,1,0:T(8,128)S(1)} %copy-done.6), kind=kLoop, calls=%fused_computation.16 | loop fusion | flops 3670014 | bytes 4718606 | tf_op jit(solution)/shard_map/jit(_where)/select_n | solution.py:423
  138.8 0.1 fusion.13
  138.9 0.1 broadcast_in_dim.152.squares
  138.9 0.0 copy-done.1
  138.9 15.3 %shard_map.137 = (f32[8,128]{1,0:T(8,128)S(1)}, bf16[4,2,32,1024]{3,2,1,0:T(8,128)(2,1)S(1)}) custom-call(f32[8,128]{1,0:T(8,128)S(1)} %broadcast_in_dim.152.squares, f32[2,128,1024]{2,1,0:T(8,128)S(1)} %get-tuple-element.37.direction, f32[2,128,1024]{2,1,0:T(8,128)S(1)} %copy-done.1), custom_call_target="tpu_custom_call" | custom-call | tf_op jit(solution)/shard_map/pallas_call | solution.py:320
  154.3 0.1 multiply_reduce_fusion.2
  154.4 1.2 subtract_select_fusion
  155.7 0.9 select_select_fusion
  (2 shorter events, 0.0 us)
Async XLA Ops:
  0.6 123.9 %copy-start = (bf16[2,128,1024]{2,1,0:T(8,128)(2,1)S(1)}, bf16[2,128,1024]{2,1,0:T(8,128)(2,1)}, u32[]{:S(2)}) copy-start(bf16[2,128,1024]{2,1,0:T(8,128)(2,1)} %param.13) | copy-start | bytes 1572868
  124.5 4.9 %copy-start.3 = (f32[2,128,1024]{2,1,0:T(8,128)S(1)}, f32[2,128,1024]{2,1,0:T(8,128)}, u32[]{:S(2)}) copy-start(f32[2,128,1024]{2,1,0:T(8,128)} %param.12) | copy-start | bytes 3145732
  129.4 4.4 %copy-start.2 = (bf16[2,4,8,32,1024]{4,3,2,1,0:T(8,128)(2,1)S(1)}, bf16[2,4,8,32,1024]{4,3,2,1,0:T(8,128)(2,1)}, u32[]{:S(2)}) copy-start(bf16[2,4,8,32,1024]{4,3,2,1,0:T(8,128)(2,1)} %get-tuple-element.10) | copy-start | bytes 12582916
  129.4 4.4 %copy-start.4 = (f32[2,128,1024]{2,1,0:T(8,128)S(1)}, f32[2,128,1024]{2,1,0:T(8,128)}, u32[]{:S(2)}) copy-start(f32[2,128,1024]{2,1,0:T(8,128)} %param.11) | copy-start | bytes 3145732
  133.9 2.6 %copy-start.5 = (f32[2,128,1024]{2,1,0:T(8,128)S(1)}, f32[2,128,1024]{2,1,0:T(8,128)}, u32[]{:S(2)}) copy-start(f32[2,128,1024]{2,1,0:T(8,128)} %param.17) | copy-start | bytes 3145732
  133.9 2.6 %copy-start.6 = (f32[2,128,1024]{2,1,0:T(8,128)S(1)}, f32[2,128,1024]{2,1,0:T(8,128)}, u32[]{:S(2)}) copy-start(f32[2,128,1024]{2,1,0:T(8,128)} %param.16) | copy-start | bytes 3145732
  133.9 5.0 %copy-start.1 = (f32[2,128,1024]{2,1,0:T(8,128)S(1)}, f32[2,128,1024]{2,1,0:T(8,128)}, u32[]{:S(2)}) copy-start(f32[2,128,1024]{2,1,0:T(8,128)} %master.1) | copy-start | bytes 3145732
